TPU v7x, 256 devices: a whole 4x4x8 slice. The times are simulated.
256 devices in a mesh: term: 32 (over z, x_lo, core), sector: 8 (over y, x_hi).
Axes of the slice: x: 4 (x_hi: 2, x_lo: 2; x = x_hi * 2 + x_lo), y: 4, z: 8, core: 2. Of those that a mesh axis runs over, the one named last changes fastest.
Arguments:
- wavefunction: bfloat16 [16, 512, 512], P('sector'), may hold values from -6 to 6
- left_operators: bfloat16 [2048, 512, 512], P(('term', 'sector')), may hold values from -0.25 to 0.25
- right_operators: bfloat16 [2048, 512, 512], P(('term', 'sector')), may hold values from -0.25 to 0.25
- source_sector: int32 [2048], P(('term', 'sector')), may hold values from 0 to 15
- target_sector: int32 [2048], P(('term', 'sector')), may hold values from 0 to 15
- live_terms: int32 [256], P(('term', 'sector')), may hold values from 1 to 8, as said below
- sector_rows: int32 [16], replicated, may hold values from 1 to 512, as said below
Outputs:
- sigma_blocks: float32 [16, 512, 512], P('sector', 'term')
Inputs may be any that keep to these rules, and one draw needn't show every extreme that they name: Term group g = term index * 8 + sector index holds the term slots g * 8 to (g + 1) * 8 - 1; its live slots are the first live_terms[g]; some group has exactly 8. `sector_rows`: some sector uses exactly 512 rows.
All inputs are finite; a program needn't handle non-finite values.
Results may differ from a plain program's by a relative error of at most 0.0029.
Values may be sent and summed in bfloat16 or wider, within the bound.
No kernel may reach another device: no remote copies, remote signals or barrier semaphores. Data moves between devices by JAX's collectives and lax.ppermute only.
A program may use at most 128 MiB of HBM per device.

v0:
```python
import jax
import jax.numpy as jnp
from jax import lax
from jax.sharding import PartitionSpec as P


def split_up(x, dim, size):
    before, after = (x.shape[:dim], x.shape[dim + 1 :])
    return jnp.moveaxis(x.reshape(*before, size, -1, *after), dim, 0)


def sum_at_owner(x, axis, dim):
    tiles = split_up(x, dim, lax.axis_size(axis))
    arrived = lax.all_to_all(tiles, axis, split_axis=0, concat_axis=0, tiled=True)
    return arrived.sum(axis=0)


def local(
    wavefunction,
    left_operators,
    right_operators,
    source_sector,
    target_sector,
    live_terms,
    sector_rows,
):
    whole_wave = lax.all_gather(wavefunction, "sector", axis=0, tiled=True)
    sector_count = whole_wave.shape[0]
    row_count = whole_wave.shape[1]
    col_count = whole_wave.shape[2]
    slot_count = left_operators.shape[0]
    row_ids = lax.iota(jnp.int32, row_count)
    live_mask = lax.iota(jnp.int32, slot_count) < live_terms[0]

    def term_product(slot):
        source_index = source_sector[slot]
        source = lax.dynamic_index_in_dim(whole_wave, source_index, 0, keepdims=False)
        keep_rows = (row_ids < sector_rows[source_index])[:, None]
        source = jnp.where(keep_rows, source, jnp.zeros_like(source))
        left_half = jnp.dot(
            left_operators[slot], source, preferred_element_type=jnp.float32
        ).astype(jnp.bfloat16)
        return lax.dot_general(
            left_half,
            right_operators[slot],
            (((1,), (1,)), ((), ())),
            preferred_element_type=jnp.float32,
        )

    partial_value = jnp.zeros((sector_count, row_count, col_count), jnp.float32)

    def apply_term(slot, partial_value):

        def contribute(partial_value):
            target_index = target_sector[slot]
            current = lax.dynamic_index_in_dim(partial_value, target_index, 0, keepdims=True)
            return lax.dynamic_update_index_in_dim(
                partial_value, current + term_product(slot)[None], target_index, 0
            )

        return lax.cond(live_mask[slot], contribute, lambda kept: kept, partial_value)

    partial_value = lax.fori_loop(0, slot_count, apply_term, partial_value)
    shares = lax.psum_scatter(partial_value, "term", scatter_dimension=1, tiled=True)
    owned = sum_at_owner(shares, "sector", 0)
    owned_sectors = owned.shape[0]
    owned_rows = owned.shape[1]
    sector_ids = lax.axis_index("sector") * owned_sectors + lax.iota(jnp.int32, owned_sectors)
    global_rows = lax.axis_index("term") * owned_rows + lax.iota(jnp.int32, owned_rows)
    limits = sector_rows[sector_ids]
    used = global_rows[None, :, None] < limits[:, None, None]
    return jnp.where(used, owned, jnp.zeros_like(owned))


def solution(mesh):
    in_specs = (
        P("sector", None, None),
        P(("term", "sector"), None, None),
        P(("term", "sector"), None, None),
        P(("term", "sector")),
        P(("term", "sector")),
        P(("term", "sector")),
        P(),
    )
    out_specs = P("sector", "term", None)
    return jax.shard_map(local, mesh=mesh, in_specs=in_specs, out_specs=out_specs, check_vma=False)
```

profile of v0, /device:TPU:6, one launch (start us, length us, event | category | flops | bytes accessed | tf_op | source)
XLA Modules:
  0.0 426.9 jit_solution(15155649393007704389)
XLA Ops:
  6.5 0.0 all-gather.2.cloned.1.call-start
  6.5 0.7 all-gather.2.cloned.1.call-update
  7.3 0.0 reduce-scatter.2.cloned.1.call-start
  8.0 0.0 copy-start
  8.0 0.0 copy-start.1
  8.0 0.0 copy-start.2
  8.0 115.5 %all-gather.2.cloned.1.call-done = bf16[16,512,512]{2,1,0:T(8,128)(2,1)} async-done(((bf16[2,512,512]{2,1,0:T(8,128)(2,1)}), bf16[16,512,512]{2,1,0:T(8,128)(2,1)}) %all-gather.2.cloned.1.call-update) | async-done | bytes 8388624 | tf_op jit(solution)/shard_map/all_gather | solution.py:27
  123.5 7.9 %broadcast_in_dim.30 = f32[16,512,512]{2,1,0:T(8,128)} broadcast(f32[]{:T(128)} %constant.61.clone.1), dimensions={} | broadcast | bytes 16777220 | tf_op jit(solution)/shard_map/broadcast_in_dim | solution.py:50
  131.4 0.0 copy-done
  131.4 0.0 copy-done.1
  131.4 0.0 copy-done.2
  131.4 30.0 %while.17 = (s32[]{:T(128)}, f32[16,512,512]{2,1,0:T(8,128)}, pred[8]{0:T(512)(128)(4,1)S(1)}, s32[8]{0:T(128)S(1)}, bf16[8,512,512]{2,1,0:T(8,128)(2,1)}, /*ind...) while((s32[]{:T(128)}, f32[16,512,512]{2,1,0:T(8,128)}, ...), condition=%wide.region_3.4_spmd.clone, body=%wide.region_0.3_spmd.clone.sunk | while | flops 537657856 | bytes 3677518 | solution.py:63
  131.5 0.6 dynamic_slice.47
  132.7 9.8 %conditional.3 = (f32[16,512,512]{2,1,0:T(8,128)}) conditional(s32[]{:T(128)} %bitcast.26, f32[16,512,512]{2,1,0:T(8,128)} %get-tuple-element.314, (s32[]{:T(128)}, s32[8]{0:T(128)S(1)}, f32[16,512,512]{2,1,0:T(8,128)}, bf16[8,512,512]{2,1,0:T(8,128)(2,1)}, s32[8]{0:T(128)S(1)}, /*index=5*/s32[16]{0:T(128)S(1)}, s32[512]{0:T(512)S(1)}, ...), branch_computations={%region_1.0_spmd, %region_2.2_spmd} | conditional | flops 537657856 | bytes 3675286 | solution.py:61
  132.7 0.6 dynamic_slice.25
  135.2 0.6 dynamic_slice.26
  135.9 0.6 broadcast_compare_fusion
  136.5 0.6 dynamic_slice.22
  139.0 3.5 fusion.3
  142.5 0.6 dynamic_slice.47
  143.7 9.8 %conditional.3 = (f32[16,512,512]{2,1,0:T(8,128)}) conditional(s32[]{:T(128)} %bitcast.26, f32[16,512,512]{2,1,0:T(8,128)} %get-tuple-element.314, (s32[]{:T(128)}, s32[8]{0:T(128)S(1)}, f32[16,512,512]{2,1,0:T(8,128)}, bf16[8,512,512]{2,1,0:T(8,128)(2,1)}, s32[8]{0:T(128)S(1)}, /*index=5*/s32[16]{0:T(128)S(1)}, s32[512]{0:T(512)S(1)}, ...), branch_computations={%region_1.0_spmd, %region_2.2_spmd} | conditional | flops 537657856 | bytes 3675286 | solution.py:61
  143.8 0.6 dynamic_slice.25
  146.3 0.6 dynamic_slice.26
  146.9 0.6 broadcast_compare_fusion
  147.5 0.6 dynamic_slice.22
  150.0 3.5 fusion.3
  153.5 0.6 dynamic_slice.47
  154.8 0.6 dynamic_slice.47
  156.2 0.6 dynamic_slice.47
  157.5 0.6 dynamic_slice.47
  158.8 0.6 dynamic_slice.47
  160.1 0.6 dynamic_slice.47
  161.4 0.0 reduce-scatter.2.cloned.1.call-update
  161.4 243.1 %reduce-scatter.2.cloned.1.call-done = f32[16,16,512]{2,1,0:T(8,128)} async-done(((f32[16,512,512]{2,1,0:T(8,128)}), f32[16,16,512]{2,1,0:T(8,128)}) %reduce-scatter.2.cloned.1.call-update) | async-done | bytes 524304 | tf_op jit(solution)/shard_map/reduce_scatter | solution.py:64
  404.6 7.3 %all-to-all-start = ((f32[8,2,16,512]{3,2,1,0:T(8,128)}), f32[8,2,16,512]{3,2,1,0:T(8,128)S(1)}, u32[]{:S(2)}, u32[]{:S(2)}) async-start(f32[8,2,16,512]{3,2,1,0:T(8,128)} %bitcast.28), calls=%async_computation.1 | async-start | bytes 1048576 | tf_op jit(solution)/shard_map/all_to_all | solution.py:14
  411.9 0.6 gather_fusion
  412.5 0.1 broadcast_compare_fusion.1
  412.6 6.8 %all-to-all-done = f32[8,2,16,512]{3,2,1,0:T(8,128)S(1)} async-done(((f32[8,2,16,512]{3,2,1,0:T(8,128)}), f32[8,2,16,512]{3,2,1,0:T(8,128)S(1)}, u32[]{:S(2)}, u32[]{:S(2)}) %all-to-all-start) | async-done | bytes 524320 | tf_op jit(solution)/shard_map/all_to_all | solution.py:14
  419.4 0.7 broadcast_select_fusion
  (19 shorter events, 0.1 us)
Async XLA Ops:
  6.5 117.0 %all-gather.2.cloned.1.call-start = ((), (), s32[]{:S(2)}) async-start(), calls=%async_computation.2 | async-start | bytes 9437184 | tf_op jit(solution)/shard_map/all_gather | solution.py:27
  7.3 397.3 %reduce-scatter.2.cloned.1.call-start = ((), (), s32[]{:S(2)}) async-start(), calls=%async_computation.3 | async-start | bytes 17301504 | tf_op jit(solution)/shard_map/reduce_scatter | solution.py:64
  8.0 123.5 %copy-start = (s32[16]{0:T(128)S(1)}, s32[16]{0:T(128)}, u32[]{:S(2)}) copy-start(s32[16]{0:T(128)} %param.17) | copy-start | bytes 196
  8.0 123.5 %copy-start.1 = (s32[8]{0:T(128)S(1)}, s32[8]{0:T(128)}, u32[]{:S(2)}) copy-start(s32[8]{0:T(128)} %param.15) | copy-start | bytes 100
  8.0 123.4 %copy-start.2 = (s32[8]{0:T(128)S(1)}, s32[8]{0:T(128)}, u32[]{:S(2)}) copy-start(s32[8]{0:T(128)} %param.14) | copy-start | bytes 100
  404.6 14.8 %all-to-all-start = ((f32[8,2,16,512]{3,2,1,0:T(8,128)}), f32[8,2,16,512]{3,2,1,0:T(8,128)S(1)}, u32[]{:S(2)}, u32[]{:S(2)}) async-start(f32[8,2,16,512]{3,2,1,0:T(8,128)} %bitcast.28), calls=%async_computation.1 | async-start | bytes 1048576 | tf_op jit(solution)/shard_map/all_to_all | solution.py:14
Sparse Core Ops, SparseCore 0:
  10.0 113.4 all-gather.1
  161.5 242.9 reduce-scatter.1
where the time goes:
time: 432 us; the launch traced here: 427 us
  waiting for transfers between devices  366 us (85%)
  local copies, waits for them, and re-layouts  17.6 us (4%)
  between operations  14.1 us (3%)
  loops' own time  12.8 us (3%)
  starting transfers between devices  7.32 us (2%)
  matrix products  6.94 us (2%)
    reduce_scatter x1, waiting for transfers between devices, local(): lax.psum_scatter(partial_value, 'term', scatter_dimension=1, tiled=True)  243 us
    all_gather x1, waiting for transfers between devices, local(): whole_wave = lax.all_gather(wavefunction, 'sector', axis=0, tiled=True)  116 us
  transfers between devices with their start and end apart: 3, of which 3 were waited for; matrix products, arithmetic and copies ran while one was open for 0% of the time, Pallas kernels for 0%

commit v1 on v0

v1 whole, which is shorter than its diff:
```python
import functools

import jax
import jax.numpy as jnp
from jax import lax
from jax.experimental import pallas as pl
from jax.experimental.pallas import tpu as pltpu
from jax.sharding import PartitionSpec as P

UNIT = 32
AXES = ("term", "sector")
DEPTH = 3


def device_index(x, y, z, core):
    x, y, z = x % 4, y % 4, z % 8
    return (z * 4 + (x % 2) * 2 + core) * 8 + y * 2 + x // 2


def pairs(move):
    every = [(x, y, z, c) for x in range(4) for y in range(4) for z in range(8) for c in range(2)]
    return [(device_index(*at), device_index(*move(*at))) for at in every]


OTHER_CORE = pairs(lambda x, y, z, c: (x, y, z, 1 - c))
FIRST_AXIS = [pairs(lambda x, y, z, c: (x + k * c, y + k * (1 - c), z, c)) for k in range(4)]
SECOND_AXIS = [pairs(lambda x, y, z, c: (x + k * (1 - c), y + k * c, z, c)) for k in range(4)]


def coordinates():
    term, sector = lax.axis_index("term"), lax.axis_index("sector")
    x_lo, core = lax.rem(lax.div(term, 2), 2), lax.rem(term, 2)
    return 2 * lax.rem(sector, 2) + x_lo, lax.div(sector, 2), lax.div(term, 4), core


def units_of(rows):
    return lax.div(rows + (UNIT - 1), UNIT)


def group_entry(core, place, i):
    along_x = 4 * lax.div(i, 2) + 2 * lax.div(place, 2) + lax.rem(i, 2)
    sector = jnp.where(core == 0, 4 * place + lax.rem(i, 4), along_x)
    first = jnp.where(core == 0, 0, lax.rem(place, 2))
    return sector, first, 1 + core


def group_count(rows_ref, core, place, i):
    sector, first, step = group_entry(core, place, i)
    count = lax.div(units_of(rows_ref[sector]) - first + step - 1, step)
    return jnp.where((core == 0) & (i >= 4), 0, jnp.maximum(count, 0))


def pack_kernel(rows_ref, wave_ref, out_ref, packed, sems):
    core = lax.rem(lax.axis_index("term"), 2)
    sector = lax.axis_index("sector")
    first_units = units_of(rows_ref[2 * sector])
    second_units = units_of(rows_ref[2 * sector + 1])

    def copy_half(half):
        lanes = pl.ds(half * 256, 256)
        for b, units, base in ((0, first_units, 0), (1, second_units, first_units)):

            @pl.loop(0, units)
            def _(u):
                at = pl.multiple_of((base + u) * UNIT, UNIT)
                packed[pl.ds(at, UNIT), :] = wave_ref[b, pl.ds(pl.multiple_of(u * UNIT, UNIT), UNIT), lanes]

    for half in range(2):
        pl.when(core == half)(functools.partial(copy_half, half))
    copies = [pltpu.make_async_copy(packed, out_ref.at[j], sems.at[j]) for j in range(out_ref.shape[0])]
    for copy in copies:
        copy.start()
    for copy in copies:
        copy.wait()


def pack_wave(sector_rows, wavefunction, rows):
    return pl.pallas_call(
        pack_kernel,
        out_shape=jax.ShapeDtypeStruct((8, rows, 256), jnp.bfloat16),
        in_specs=[pl.BlockSpec(memory_space=pltpu.SMEM), pl.BlockSpec(memory_space=pltpu.VMEM)],
        out_specs=pl.BlockSpec(memory_space=pl.ANY),
        scratch_shapes=[pltpu.VMEM((rows, 256), jnp.bfloat16), pltpu.SemaphoreType.DMA((8,))],
        compiler_params=pltpu.CompilerParams(vmem_limit_bytes=24 * 1024 * 1024),
        name="pack_wave",
    )(sector_rows, wavefunction)


def terms_kernel(
    wave_rows,
    rows_ref,
    source_ref,
    target_ref,
    live_ref,
    far_ref,
    near_wave,
    far_wave,
    near_left,
    near_right,
    far_left,
    far_right,
    own_ref,
    send1,
    send2,
    send3,
    acc,
    left_buf,
    right_buf,
    wave_buf,
    half_buf,
    sems,
):
    x, y, _, core = coordinates()
    near_live = live_ref[0]
    total = near_live + far_ref[16]
    last_start = 8 * wave_rows - 512

    def facts(i):
        near = i < near_live
        slot = jnp.where(near, i, i - near_live)
        source = jnp.where(near, source_ref[slot], far_ref[slot])
        target = jnp.where(near, target_ref[slot], far_ref[8 + slot])
        return near, slot, source, target

    def wave_place(source):
        pair = lax.div(source, 2)
        before = jnp.where(lax.rem(source, 2) == 1, units_of(rows_ref[2 * pair]), 0) * UNIT
        want = pair * wave_rows + before
        start = jnp.minimum(want, last_start)
        return pl.multiple_of(start, UNIT), pl.multiple_of(want - start, UNIT)

    def copies(near, slot, source, buf):
        start, _ = wave_place(source)
        left = near_left if near else far_left
        right = near_right if near else far_right
        lanes = pl.ds(pl.multiple_of(core * 256, 256), 256)
        return (
            pltpu.make_async_copy(left.at[slot], left_buf.at[buf], sems.at[buf, 0]),
            pltpu.make_async_copy(right.at[slot, lanes], right_buf.at[buf], sems.at[buf, 1]),
            pltpu.make_async_copy(
                near_wave.at[pl.ds(start, 512)], wave_buf.at[buf, 0, pl.ds(0, 512)], sems.at[buf, 2]
            ),
            pltpu.make_async_copy(
                far_wave.at[pl.ds(start, 512)], wave_buf.at[buf, 1, pl.ds(0, 512)], sems.at[buf, 3]
            ),
        )

    def begin(i):
        near, slot, source, _ = facts(i)
        buf = lax.rem(i, DEPTH)

        @pl.when(near)
        def _():
            for copy in copies(True, slot, source, buf):
                copy.start()

        @pl.when(jnp.logical_not(near))
        def _():
            for copy in copies(False, slot, source, buf):
                copy.start()

    for i in range(DEPTH - 1):
        pl.when(i < total)(functools.partial(begin, i))

    for q in range(16):

        @pl.loop(0, units_of(rows_ref[q]))
        def _(u):
            acc[pl.ds(pl.multiple_of(q * 512 + u * UNIT, UNIT), UNIT), :] = jnp.zeros((UNIT, 256), jnp.float32)

    @pl.loop(0, total)
    def _(i):
        pl.when(i + DEPTH - 1 < total)(lambda: begin(i + DEPTH - 1))
        near, slot, source, target = facts(i)
        buf = lax.rem(i, DEPTH)
        for copy in copies(True, slot, source, buf):
            copy.wait()
        _, shift = wave_place(source)
        source_rows = rows_ref[source]
        target_rows = rows_ref[target]

        def product(row, depth):
            keep = lax.broadcasted_iota(jnp.int32, (depth, 1), 0) < source_rows
            left = left_buf[buf, pl.ds(row, 256), pl.ds(0, depth)]
            for wave_half in range(2):
                wave = wave_buf[buf, wave_half, pl.ds(shift, depth), :]
                wave = jnp.where(keep, wave, jnp.zeros_like(wave))
                half = jnp.dot(left, wave, preferred_element_type=jnp.float32)
                half_buf[wave_half] = half.astype(jnp.bfloat16)
            for low in range(2):

                @pl.when(core == low)
                def _():
                    halves = (half_buf[low], half_buf[1 - low])
                    both = jnp.concatenate(halves, axis=1)
                    out = lax.dot_general(
                        both, right_buf[buf], (((1,), (1,)), ((), ())), preferred_element_type=jnp.float32
                    )
                    at = pl.ds(pl.multiple_of(target * 512 + row, 256), 256)
                    acc[at, :] += out

        for row in range(0, 512, 256):
            pl.when((target_rows > row) & (source_rows <= 256))(functools.partial(product, row, 256))
            pl.when((target_rows > row) & (source_rows > 256))(functools.partial(product, row, 512))

    place = jnp.where(core == 0, y, x)
    for k, dest in enumerate((own_ref, send1, send2, send3)):
        there = lax.rem(place + k, 4)

        def one_sector(i, filled):
            sector, first, step = group_entry(core, there, i)
            count = group_count(rows_ref, core, there, i)

            @pl.loop(0, count)
            def _(j):
                at = pl.multiple_of(sector * 512 + (first + step * j) * UNIT, UNIT)
                to = pl.multiple_of((filled + j) * UNIT, UNIT)
                dest[pl.ds(to, UNIT), :] = acc[pl.ds(at, UNIT), :].astype(dest.dtype)

            return filled + count

        lax.fori_loop(0, 8, one_sector, 0)


def term_products(rows, small, far_small, near_wave, far_wave, near_left, near_right, far_left, far_right, group_rows):
    wave_rows = near_wave.shape[0] // 8
    smem = pl.BlockSpec(memory_space=pltpu.SMEM)
    hbm = pl.BlockSpec(memory_space=pl.ANY)
    vmem = pl.BlockSpec(memory_space=pltpu.VMEM)
    send = jax.ShapeDtypeStruct((group_rows, 256), jnp.bfloat16)
    return pl.pallas_call(
        functools.partial(terms_kernel, wave_rows),
        out_shape=(jax.ShapeDtypeStruct((group_rows, 256), jnp.float32), send, send, send),
        in_specs=[smem] * 5 + [hbm] * 6,
        out_specs=(vmem,) * 4,
        scratch_shapes=[
            pltpu.VMEM((16 * 512, 256), jnp.float32),
            pltpu.VMEM((DEPTH, 512, 512), jnp.bfloat16),
            pltpu.VMEM((DEPTH, 256, 512), jnp.bfloat16),
            pltpu.VMEM((DEPTH, 2, 1024, 256), jnp.bfloat16),
            pltpu.VMEM((2, 256, 256), jnp.bfloat16),
            pltpu.SemaphoreType.DMA((DEPTH, 4)),
        ],
        compiler_params=pltpu.CompilerParams(vmem_limit_bytes=48 * 1024 * 1024),
        cost_estimate=pl.CostEstimate(flops=8 * 10**9, bytes_accessed=16 * 2**20, transcendentals=0),
        name="term_products",
    )(rows, *small, far_small, near_wave, far_wave, near_left, near_right, far_left, far_right)


def regroup_kernel(rows_ref, own_ref, got1, got2, got3, keep_ref, send1, send2, send3, blocks):
    x, y, _, core = coordinates()
    place, other = jnp.where(core == 0, y, x), jnp.where(core == 0, x, y)
    blocks[...] = jnp.zeros_like(blocks)

    def one_sector(i, filled):
        _, first, step = group_entry(core, place, i)
        count = group_count(rows_ref, core, place, i)

        @pl.loop(0, count)
        def _(j):
            unit = first + step * j
            at = pl.ds(pl.multiple_of((filled + j) * UNIT, UNIT), UNIT)
            total = own_ref[at, :] + got1[at, :].astype(jnp.float32)
            total = total + got2[at, :].astype(jnp.float32)
            total = total + got3[at, :].astype(jnp.float32)
            there = jnp.where(core == 0, 2 * lax.div(i, 2) + lax.rem(unit, 2), lax.div(i, 2))
            k = lax.rem(there - other + 4, 4)
            to = pl.multiple_of((lax.rem(i, 2) * 8 + lax.div(unit, 2)) * UNIT, UNIT)
            blocks[k, pl.ds(to, UNIT), :] = total

        return filled + count

    lax.fori_loop(0, 8, one_sector, 0)
    keep_ref[...] = blocks[0]
    for k, dest in enumerate((send1, send2, send3)):
        dest[...] = blocks[k + 1].astype(jnp.bfloat16)


def regroup(rows, own, got):
    vmem = pl.BlockSpec(memory_space=pltpu.VMEM)
    send = jax.ShapeDtypeStruct((512, 256), jnp.bfloat16)
    return pl.pallas_call(
        regroup_kernel,
        out_shape=(jax.ShapeDtypeStruct((512, 256), jnp.float32), send, send, send),
        in_specs=[pl.BlockSpec(memory_space=pltpu.SMEM)] + [vmem] * 4,
        out_specs=(vmem,) * 4,
        scratch_shapes=[pltpu.VMEM((4, 512, 256), jnp.float32)],
        compiler_params=pltpu.CompilerParams(vmem_limit_bytes=32 * 1024 * 1024),
        name="regroup",
    )(rows, own, *got)


def spread_kernel(keep_ref, got1, got2, got3, out_ref):
    total = keep_ref[...] + got1[...].astype(jnp.float32)
    total = total + got2[...].astype(jnp.float32)
    total = (total + got3[...].astype(jnp.float32)).astype(jnp.bfloat16)
    for b in range(2):
        for z in range(8):
            for core in range(2):
                start = (b * 8 + z) * UNIT + core * 16
                out_ref[z * 2 + core, b] = total[start : start + 16]


def spread(keep, got):
    vmem = pl.BlockSpec(memory_space=pltpu.VMEM)
    return pl.pallas_call(
        spread_kernel,
        out_shape=jax.ShapeDtypeStruct((16, 2, 16, 256), jnp.bfloat16),
        in_specs=[vmem] * 4,
        out_specs=vmem,
        name="spread",
    )(keep, *got)


def finish_kernel(rows_ref, parts_ref, out_ref):
    term, sector = lax.axis_index("term"), lax.axis_index("sector")
    row = term * 16 + lax.broadcasted_iota(jnp.int32, (16, 1), 0)
    for b in range(2):
        used = row < rows_ref[2 * sector + b]
        for half in range(2):
            total = parts_ref[half, b].astype(jnp.float32)
            for z in range(1, 8):
                total = total + parts_ref[z * 2 + half, b].astype(jnp.float32)
            out_ref[b, :, half * 256 : half * 256 + 256] = jnp.where(used, total, jnp.zeros_like(total))


def finish(rows, parts):
    vmem = pl.BlockSpec(memory_space=pltpu.VMEM)
    return pl.pallas_call(
        finish_kernel,
        out_shape=jax.ShapeDtypeStruct((2, 16, 512), jnp.float32),
        in_specs=[pl.BlockSpec(memory_space=pltpu.SMEM), vmem],
        out_specs=vmem,
        name="finish",
    )(rows, parts)


def local(
    wavefunction,
    left_operators,
    right_operators,
    source_sector,
    target_sector,
    live_terms,
    sector_rows,
    wave_rows=1024,
    group_rows=2048,
):
    swap = functools.partial(lax.ppermute, axis_name=AXES, perm=OTHER_CORE)
    far_small = swap(jnp.concatenate([source_sector, target_sector, live_terms]))
    far_left, far_right = swap(left_operators), swap(right_operators)
    packed = pack_wave(sector_rows, wavefunction, wave_rows)
    near_wave = lax.all_to_all(packed, "sector", split_axis=0, concat_axis=0, tiled=True)
    far_wave = swap(near_wave)
    small = (source_sector, target_sector, live_terms)
    own, *sends = term_products(
        sector_rows,
        small,
        far_small,
        near_wave.reshape(-1, 256),
        far_wave.reshape(-1, 256),
        left_operators,
        right_operators,
        far_left,
        far_right,
        group_rows,
    )
    got = [lax.ppermute(s, AXES, FIRST_AXIS[k + 1]) for k, s in enumerate(sends)]
    keep, *sends = regroup(sector_rows, own, got)
    got = [lax.ppermute(s, AXES, SECOND_AXIS[k + 1]) for k, s in enumerate(sends)]
    parts = spread(keep, got)
    groups = [[z * 4 + x_lo * 2 + core for z in range(8) for core in range(2)] for x_lo in range(2)]
    arrived = lax.all_to_all(
        parts, "term", split_axis=0, concat_axis=0, axis_index_groups=groups, tiled=True
    )
    return finish(sector_rows, arrived)


def solution(mesh):
    in_specs = (
        P("sector", None, None),
        P(("term", "sector"), None, None),
        P(("term", "sector"), None, None),
        P(("term", "sector")),
        P(("term", "sector")),
        P(("term", "sector")),
        P(),
    )
    out_specs = P("sector", "term", None)
    return jax.shard_map(local, mesh=mesh, in_specs=in_specs, out_specs=out_specs, check_vma=False)
```

time: 432 us -> 149 us (0.34)
  waiting for transfers between devices: 366 us -> 85.3 us
  blocking collectives: 0 us -> 19.1 us
  starting transfers between devices: 7.32 us -> 23 us
  between operations: 14.1 us -> 0.73 us
  loops' own time: 12.8 us -> 0 us
  Pallas kernels: 0 us -> 11.3 us
  local copies, waits for them, and re-layouts: 17.6 us -> 7.27 us
  matrix products: 6.94 us -> 0 us
    reduce_scatter x1 -> x0, waiting for transfers between devices: 243 us -> none  [local(): lax.psum_scatter(partial_value, 'term', scatter_dimension=1, tiled=True)]
    all_gather x1 -> x0, waiting for transfers between devices: 116 us -> none  [local(): whole_wave = lax.all_gather(wavefunction, 'sector', axis=0, tiled=True)]
    all_to_all x1, waiting for transfers between devices: 6.79 us -> 47.8 us  [local(): lax.all_to_all(packed, 'sector', split_axis=0, concat_axis=0, tiled=True)]
    ppermute x0 -> x10, waiting for transfers between devices: none -> 37.5 us  [the longest x3 24 us: local(): lax.ppermute(s, AXES, FIRST_AXIS[k + 1])]
    all_to_all x0 -> x1, blocking collectives: none -> 19.1 us  [local(): lax.all_to_all(parts, 'term', split_axis=0, concat_axis=0, axis_index_gro...]
    ppermute x0 -> x10, starting transfers between devices: none -> 15.3 us  [the longest x3 11 us: local(): lax.ppermute(s, AXES, FIRST_AXIS[k + 1])]
    another operation x9 -> x0, loops' own time: 12.8 us -> none  [the longest x8 7.58 us: apply_term(): lax.cond(live_mask[slot], contribute, lambda kept: kept, partial_value)]
    pallas_call x0 -> x5, Pallas kernels: none -> 11.3 us  [the longest x1 5.21 us: term_products(): pl.pallas_call(functools.partial(terms_kernel, wave_rows), out_shape=(jax...]
  transfers between devices with their start and end apart: 3 -> 11, of which waited for: 3 -> 8; matrix products, arithmetic and copies ran while one was open for 0% -> 0% of each run, Pallas kernels for 0% -> 0%
where the time goes in v1:
time: 149 us; the launch traced here: 147 us
  waiting for transfers between devices  85.3 us (57%)
  starting transfers between devices  23 us (15%)
  blocking collectives  19.1 us (13%)
  Pallas kernels  11.3 us (8%)
  local copies, waits for them, and re-layouts  7.27 us (5%)
    all_to_all x1, waiting for transfers between devices, local(): lax.all_to_all(packed, 'sector', split_axis=0, concat_axis=0, tiled=True)  47.8 us
    ppermute x3, waiting for transfers between devices, local(): lax.ppermute(s, AXES, FIRST_AXIS[k + 1])  24 us
    all_to_all x1, blocking collectives, local(): lax.all_to_all(parts, 'term', split_axis=0, concat_axis=0, axis_index_gro...  19.1 us
    ppermute x3, starting transfers between devices, local(): lax.ppermute(s, AXES, FIRST_AXIS[k + 1])  11 us
    all_to_all x1, starting transfers between devices, local(): lax.all_to_all(packed, 'sector', split_axis=0, concat_axis=0, tiled=True)  7.66 us
    ppermute x3, waiting for transfers between devices, local(): lax.ppermute(s, AXES, SECOND_AXIS[k + 1])  7.39 us
    unnamed x22, local copies, waits for them, and re-layouts  7.27 us
    ppermute x1, waiting for transfers between devices, local(): swap(jnp.concatenate([source_sector, target_sector, live_terms]))  5.83 us
  transfers between devices with their start and end apart: 11, of which 8 were waited for; matrix products, arithmetic and copies ran while one was open for 0% of the time, Pallas kernels for 0%

profile of v1, /device:TPU:6, one launch (start us, length us, event | category | flops | bytes accessed | tf_op | source)
XLA Modules:
  0.0 146.8 jit_solution(3204021233413602502)
XLA Ops:
  0.0 0.0 copy-start.1
  0.0 1.2 copy-done.1
  1.2 0.0 copy-start.3
  1.2 0.7 copy-done.3
  1.9 1.0 pack_wave.1
  2.9 0.0 copy-start
  2.9 1.9 %copy-done = bf16[8,1024,256]{2,1,0:T(8,128)(2,1)} copy-done((bf16[8,1024,256]{2,1,0:T(8,128)(2,1)}, bf16[8,1024,256]{2,1,0:T(8,128)(2,1)S(1)}, u32[]{:S(2)}) %copy-start) | copy-done | bytes 4194328
  4.8 0.0 copy-start.5
  4.8 0.0 copy-start.6
  4.8 0.0 copy-start.4
  4.8 7.7 %all-to-all-start = ((bf16[8,1024,256]{2,1,0:T(8,128)(2,1)}), bf16[8,1024,256]{2,1,0:T(8,128)(2,1)}, u32[]{:S(2)}, u32[]{:S(2)}) async-start(bf16[8,1024,256]{2,1,0:T(8,128)(2,1)} %copy-done), calls=%async_computation | async-start | bytes 8388608 | tf_op jit(solution)/shard_map/all_to_all | solution.py:353
  12.5 0.0 collective-permute-start.2
  12.5 0.5 collective-permute-start.3
  13.0 47.8 %all-to-all-done = bf16[8,1024,256]{2,1,0:T(8,128)(2,1)} async-done(((bf16[8,1024,256]{2,1,0:T(8,128)(2,1)}), bf16[8,1024,256]{2,1,0:T(8,128)(2,1)}, u32[]{:S(2)}, u32[]{:S(2)}) %all-to-all-start) | async-done | bytes 4194336 | tf_op jit(solution)/shard_map/all_to_all | solution.py:353
  60.8 0.0 collective-permute-start.1
  61.5 0.0 copy-done.5
  61.5 0.0 copy-done.6
  61.5 0.1 pad_add_fusion
  61.6 0.5 collective-permute-start
  62.1 5.8 %collective-permute-done.far_ref = s32[17]{0:T(128)S(1)} collective-permute-done((s32[17]{0:T(128)S(1)}, s32[17]{0:T(128)S(1)}, u32[]{:S(2)}, u32[]{:S(2)}) %collective-permute-start) | collective-permute-done | bytes 100 | tf_op jit(solution)/shard_map/ppermute | solution.py:350
  67.9 0.0 collective-permute-done.2.far_left
  68.0 0.0 collective-permute-done.3.far_right
  68.0 0.2 collective-permute-done.1
  68.2 0.0 copy-start.10
  68.2 1.9 %copy-done.10 = bf16[8,1024,256]{2,1,0:T(8,128)(2,1)} copy-done((bf16[8,1024,256]{2,1,0:T(8,128)(2,1)}, bf16[8,1024,256]{2,1,0:T(8,128)(2,1)S(1)}, u32[]{:S(2)}) %copy-start.10) | copy-done | bytes 4194328
  70.1 0.0 copy-done.4
  70.1 5.2 %term_products.1 = (f32[2048,256]{1,0:T(8,128)S(1)}, bf16[2048,256]{1,0:T(8,128)(2,1)S(1)}, bf16[2048,256]{1,0:T(8,128)(2,1)S(1)}, bf16[2048,256]{1,0:T(8,128)(2,1)S(1)}) custom-call(s32[16]{0:T(128)S(1)} %copy-done.4, s32[8]{0:T(128)S(1)} %copy-done.5, s32[8]{0:T(128)S(1)} %copy-done.6, s32[1]{0:T(128)S(6)} %copy.8.live_ref, ...), custom_call_target="tpu_custom_call" | custom-call | flops 8000000000 | bytes 16777216 | tf_op jit(solution)/shard_map/term_products/pallas_call | solution.py:231
  75.4 3.9 %collective-permute-start.4 = (bf16[2048,256]{1,0:T(8,128)(2,1)S(1)}, bf16[2048,256]{1,0:T(8,128)(2,1)S(1)}, u32[]{:S(2)}, u32[]{:S(2)}) collective-permute-start(bf16[2048,256]{1,0:T(8,128)(2,1)S(1)} %get-tuple-element.14), channel_id=1, source_target_pairs={{0,2},{8,24},{32,34},{40,56},{64,66},{72,88},{96,98},{104,120},{12... | collective-permute-start | bytes 3145736 | tf_op jit(solution)/shard_map/ppermute | solution.py:368
  79.2 7.1 %collective-permute-start.5 = (bf16[2048,256]{1,0:T(8,128)(2,1)S(1)}, bf16[2048,256]{1,0:T(8,128)(2,1)S(1)}, u32[]{:S(2)}, u32[]{:S(2)}) collective-permute-start(bf16[2048,256]{1,0:T(8,128)(2,1)S(1)} %get-tuple-element.15), channel_id=1, source_target_pairs={{0,4},{8,9},{32,36},{40,41},{64,68},{72,73},{96,100},{104,105},{12... | collective-permute-start | bytes 3145736 | tf_op jit(solution)/shard_map/ppermute | solution.py:368
  86.3 0.0 collective-permute-start.6
  86.3 11.3 %collective-permute-done.4.got1 = bf16[2048,256]{1,0:T(8,128)(2,1)S(1)} collective-permute-done((bf16[2048,256]{1,0:T(8,128)(2,1)S(1)}, bf16[2048,256]{1,0:T(8,128)(2,1)S(1)}, u32[]{:S(2)}, u32[]{:S(2)}) %collective-permute-start.4) | collective-permute-done | bytes 1048608 | tf_op jit(solution)/shard_map/ppermute | solution.py:368
  97.7 12.7 %collective-permute-done.5.got2 = bf16[2048,256]{1,0:T(8,128)(2,1)S(1)} collective-permute-done((bf16[2048,256]{1,0:T(8,128)(2,1)S(1)}, bf16[2048,256]{1,0:T(8,128)(2,1)S(1)}, u32[]{:S(2)}, u32[]{:S(2)}) %collective-permute-start.5) | collective-permute-done | bytes 1048608 | tf_op jit(solution)/shard_map/ppermute | solution.py:368
  110.3 0.0 collective-permute-done.6.got3
  110.4 1.4 regroup.1
  111.8 0.0 copy-start.2
  111.8 0.8 copy-done.2
  112.6 0.0 collective-permute-start.7
  112.6 1.9 %collective-permute-start.8 = (bf16[512,256]{1,0:T(8,128)(2,1)S(1)}, bf16[512,256]{1,0:T(8,128)(2,1)S(1)}, u32[]{:S(2)}, u32[]{:S(2)}) collective-permute-start(bf16[512,256]{1,0:T(8,128)(2,1)S(1)} %get-tuple-element.19), channel_id=1, source_target_pairs={{0,1},{8,12},{32,33},{40,44},{64,65},{72,76},{96,97},{104,108},{12... | collective-permute-start | bytes 786440 | tf_op jit(solution)/shard_map/ppermute | solution.py:370
  114.4 1.4 collective-permute-start.9
  115.9 3.1 %collective-permute-done.7.got1 = bf16[512,256]{1,0:T(8,128)(2,1)S(1)} collective-permute-done((bf16[512,256]{1,0:T(8,128)(2,1)S(1)}, bf16[512,256]{1,0:T(8,128)(2,1)S(1)}, u32[]{:S(2)}, u32[]{:S(2)}) %collective-permute-start.7) | collective-permute-done | bytes 262176 | tf_op jit(solution)/shard_map/ppermute | solution.py:370
  118.9 0.0 copy-start.7
  119.0 1.6 %collective-permute-done.8.got2 = bf16[512,256]{1,0:T(8,128)(2,1)S(1)} collective-permute-done((bf16[512,256]{1,0:T(8,128)(2,1)S(1)}, bf16[512,256]{1,0:T(8,128)(2,1)S(1)}, u32[]{:S(2)}, u32[]{:S(2)}) %collective-permute-start.8) | collective-permute-done | bytes 262176 | tf_op jit(solution)/shard_map/ppermute | solution.py:370
  120.6 0.0 copy-start.8
  120.6 2.7 %collective-permute-done.9.got3 = bf16[512,256]{1,0:T(8,128)(2,1)S(1)} collective-permute-done((bf16[512,256]{1,0:T(8,128)(2,1)S(1)}, bf16[512,256]{1,0:T(8,128)(2,1)S(1)}, u32[]{:S(2)}, u32[]{:S(2)}) %collective-permute-start.9) | collective-permute-done | bytes 262176 | tf_op jit(solution)/shard_map/ppermute | solution.py:370
  123.3 0.0 copy-start.9
  123.3 0.0 copy-done.7
  123.3 0.0 copy-done.8
  123.3 0.7 copy-done.9
  124.0 2.1 %spread.1 = bf16[16,2,16,256]{3,2,1,0:T(8,128)(2,1)} custom-call(f32[512,256]{1,0:T(8,128)} %copy-done.2, bf16[512,256]{1,0:T(8,128)(2,1)} %copy-done.7, bf16[512,256]{1,0:T(8,128)(2,1)} %copy-done.8, bf16[512,256]{1,0:T(8,128)(2,1)} %copy-done.9), custom_call_target="tpu_custom_call" | custom-call | tf_op jit(solution)/shard_map/spread/pallas_call | solution.py:306
  126.0 19.1 %all_to_all.10.parts_ref = bf16[16,2,16,256]{3,2,1,0:T(8,128)(2,1)} all-to-all(bf16[16,2,16,256]{3,2,1,0:T(8,128)(2,1)} %spread.1), channel_id=1, replica_groups={{0,8,32,40,64,72,96,104,128,136,160,168,192,200,224,232},{16,24,48,56,8..., dimensions={0} | all-to-all | bytes 524288 | tf_op jit(solution)/shard_map/all_to_all | solution.py:373
  145.2 1.6 %finish.1 = f32[2,16,512]{2,1,0:T(8,128)} custom-call(s32[16]{0:T(128)} %rows_ref.7, bf16[16,2,16,256]{3,2,1,0:T(8,128)(2,1)} %all_to_all.10.parts_ref), custom_call_target="tpu_custom_call" | custom-call | tf_op jit(solution)/shard_map/finish/pallas_call | solution.py:329
Async XLA Ops:
  0.0 1.2 copy-start.1
  1.2 0.7 copy-start.3
  2.9 1.9 %copy-start = (bf16[8,1024,256]{2,1,0:T(8,128)(2,1)}, bf16[8,1024,256]{2,1,0:T(8,128)(2,1)S(1)}, u32[]{:S(2)}) copy-start(bf16[8,1024,256]{2,1,0:T(8,128)(2,1)S(1)} %pack_wave.1) | copy-start | bytes 12582916
  4.8 56.7 %copy-start.5 = (s32[8]{0:T(128)S(1)}, s32[8]{0:T(128)}, u32[]{:S(2)}) copy-start(s32[8]{0:T(128)} %source_ref.1) | copy-start | bytes 100
  4.8 56.7 %copy-start.6 = (s32[8]{0:T(128)S(1)}, s32[8]{0:T(128)}, u32[]{:S(2)}) copy-start(s32[8]{0:T(128)} %target_ref.1) | copy-start | bytes 100
  4.8 65.3 %copy-start.4 = (s32[16]{0:T(128)S(1)}, s32[16]{0:T(128)}, u32[]{:S(2)}) copy-start(s32[16]{0:T(128)} %rows_ref.7) | copy-start | bytes 196
  4.8 56.0 %all-to-all-start = ((bf16[8,1024,256]{2,1,0:T(8,128)(2,1)}), bf16[8,1024,256]{2,1,0:T(8,128)(2,1)}, u32[]{:S(2)}, u32[]{:S(2)}) async-start(bf16[8,1024,256]{2,1,0:T(8,128)(2,1)} %copy-done), calls=%async_computation | async-start | bytes 8388608 | tf_op jit(solution)/shard_map/all_to_all | solution.py:353
  12.5 55.5 %collective-permute-start.2 = (bf16[8,512,512]{2,1,0:T(8,128)(2,1)}, bf16[8,512,512]{2,1,0:T(8,128)(2,1)}, u32[]{:S(2)}, u32[]{:S(2)}) collective-permute-start(bf16[8,512,512]{2,1,0:T(8,128)(2,1)} %near_left.1), channel_id=1, source_target_pairs={{0,8},{8,0},{32,40},{40,32},{64,72},{72,64},{96,104},{104,96},{128... | collective-permute-start | bytes 12582920 | tf_op jit(solution)/shard_map/ppermute | solution.py:351
  12.5 55.5 %collective-permute-start.3 = (bf16[8,512,512]{2,1,0:T(8,128)(2,1)}, bf16[8,512,512]{2,1,0:T(8,128)(2,1)}, u32[]{:S(2)}, u32[]{:S(2)}) collective-permute-start(bf16[8,512,512]{2,1,0:T(8,128)(2,1)} %near_right.1), channel_id=1, source_target_pairs={{0,8},{8,0},{32,40},{40,32},{64,72},{72,64},{96,104},{104,96},{128... | collective-permute-start | bytes 12582920 | tf_op jit(solution)/shard_map/ppermute | solution.py:351
  60.8 7.4 %collective-permute-start.1 = (bf16[8,1024,256]{2,1,0:T(8,128)(2,1)}, bf16[8,1024,256]{2,1,0:T(8,128)(2,1)S(1)}, u32[]{:S(2)}, u32[]{:S(2)}) collective-permute-start(bf16[8,1024,256]{2,1,0:T(8,128)(2,1)} %all-to-all-done), channel_id=1, source_target_pairs={{0,8},{8,0},{32,40},{40,32},{64,72},{72,64},{96,104},{104,96},{128... | collective-permute-start | bytes 12582920 | tf_op jit(solution)/shard_map/ppermute | solution.py:354
  61.6 6.4 %collective-permute-start = (s32[17]{0:T(128)S(1)}, s32[17]{0:T(128)S(1)}, u32[]{:S(2)}, u32[]{:S(2)}) collective-permute-start(s32[17]{0:T(128)S(1)} %pad_add_fusion), channel_id=1, source_target_pairs={{0,8},{8,0},{32,40},{40,32},{64,72},{72,64},{96,104},{104,96},{128... | collective-permute-start | bytes 212 | tf_op jit(solution)/shard_map/ppermute | solution.py:350
  68.2 1.9 %copy-start.10 = (bf16[8,1024,256]{2,1,0:T(8,128)(2,1)}, bf16[8,1024,256]{2,1,0:T(8,128)(2,1)S(1)}, u32[]{:S(2)}) copy-start(bf16[8,1024,256]{2,1,0:T(8,128)(2,1)S(1)} %collective-permute-done.1) | copy-start | bytes 12582916
  75.4 22.3 %collective-permute-start.4 = (bf16[2048,256]{1,0:T(8,128)(2,1)S(1)}, bf16[2048,256]{1,0:T(8,128)(2,1)S(1)}, u32[]{:S(2)}, u32[]{:S(2)}) collective-permute-start(bf16[2048,256]{1,0:T(8,128)(2,1)S(1)} %get-tuple-element.14), channel_id=1, source_target_pairs={{0,2},{8,24},{32,34},{40,56},{64,66},{72,88},{96,98},{104,120},{12... | collective-permute-start | bytes 3145736 | tf_op jit(solution)/shard_map/ppermute | solution.py:368
  79.2 31.1 %collective-permute-start.5 = (bf16[2048,256]{1,0:T(8,128)(2,1)S(1)}, bf16[2048,256]{1,0:T(8,128)(2,1)S(1)}, u32[]{:S(2)}, u32[]{:S(2)}) collective-permute-start(bf16[2048,256]{1,0:T(8,128)(2,1)S(1)} %get-tuple-element.15), channel_id=1, source_target_pairs={{0,4},{8,9},{32,36},{40,41},{64,68},{72,73},{96,100},{104,105},{12... | collective-permute-start | bytes 3145736 | tf_op jit(solution)/shard_map/ppermute | solution.py:368
  86.3 24.0 %collective-permute-start.6 = (bf16[2048,256]{1,0:T(8,128)(2,1)S(1)}, bf16[2048,256]{1,0:T(8,128)(2,1)S(1)}, u32[]{:S(2)}, u32[]{:S(2)}) collective-permute-start(bf16[2048,256]{1,0:T(8,128)(2,1)S(1)} %get-tuple-element.16), channel_id=1, source_target_pairs={{0,6},{8,25},{32,38},{40,57},{64,70},{72,89},{96,102},{104,121},{1... | collective-permute-start | bytes 3145736 | tf_op jit(solution)/shard_map/ppermute | solution.py:368
  111.8 0.8 copy-start.2
  112.6 6.4 %collective-permute-start.7 = (bf16[512,256]{1,0:T(8,128)(2,1)S(1)}, bf16[512,256]{1,0:T(8,128)(2,1)S(1)}, u32[]{:S(2)}, u32[]{:S(2)}) collective-permute-start(bf16[512,256]{1,0:T(8,128)(2,1)S(1)} %get-tuple-element.18), channel_id=1, source_target_pairs={{0,16},{8,10},{32,48},{40,42},{64,80},{72,74},{96,112},{104,106},{... | collective-permute-start | bytes 786440 | tf_op jit(solution)/shard_map/ppermute | solution.py:370
  112.6 8.0 %collective-permute-start.8 = (bf16[512,256]{1,0:T(8,128)(2,1)S(1)}, bf16[512,256]{1,0:T(8,128)(2,1)S(1)}, u32[]{:S(2)}, u32[]{:S(2)}) collective-permute-start(bf16[512,256]{1,0:T(8,128)(2,1)S(1)} %get-tuple-element.19), channel_id=1, source_target_pairs={{0,1},{8,12},{32,33},{40,44},{64,65},{72,76},{96,97},{104,108},{12... | collective-permute-start | bytes 786440 | tf_op jit(solution)/shard_map/ppermute | solution.py:370
  114.4 8.8 %collective-permute-start.9 = (bf16[512,256]{1,0:T(8,128)(2,1)S(1)}, bf16[512,256]{1,0:T(8,128)(2,1)S(1)}, u32[]{:S(2)}, u32[]{:S(2)}) collective-permute-start(bf16[512,256]{1,0:T(8,128)(2,1)S(1)} %get-tuple-element.20), channel_id=1, source_target_pairs={{0,17},{8,14},{32,49},{40,46},{64,81},{72,78},{96,113},{104,110},{... | collective-permute-start | bytes 786440 | tf_op jit(solution)/shard_map/ppermute | solution.py:370
  118.9 4.3 %copy-start.7 = (bf16[512,256]{1,0:T(8,128)(2,1)}, bf16[512,256]{1,0:T(8,128)(2,1)S(1)}, u32[]{:S(2)}) copy-start(bf16[512,256]{1,0:T(8,128)(2,1)S(1)} %collective-permute-done.7.got1) | copy-start | bytes 786436
  120.6 2.7 %copy-start.8 = (bf16[512,256]{1,0:T(8,128)(2,1)}, bf16[512,256]{1,0:T(8,128)(2,1)S(1)}, u32[]{:S(2)}) copy-start(bf16[512,256]{1,0:T(8,128)(2,1)S(1)} %collective-permute-done.8.got2) | copy-start | bytes 786436
  123.3 0.7 copy-start.9
